TPU v7x, 256 devices: a whole 4x4x8 slice. The times are simulated.
256 devices in a mesh: beam: 8 (over x, core), row: 32 (over y, z).
Axes of the slice: x: 4, y: 4, z: 8, core: 2. Of those that a mesh axis runs over, the one named last changes fastest.
Arguments:
- dirty: float32 [8, 2048, 2048], P('beam', 'row'), may hold values from -6 to 6
- model: bfloat16 [8, 2048, 2048], P('beam', 'row'), may hold values from -6 to 6
- psf_spectrum: float32 [8, 2, 2048, 2048], P('beam', None, None, 'row'), may hold values from -4 to 4
- primary_beam: bfloat16 [8, 2048, 2048], P('beam', 'row'), may hold values from 0.049804688 to 1
- offsets: int32 [8], replicated, may hold values from 0 to 16
Outputs:
- residual: float32 [8, 2048, 2048], P('beam', 'row')
- returned: float32 [8, 2048, 2048], P('beam', 'row')
All inputs are finite; a program needn't handle non-finite values.
Results may differ from a plain program's by a relative error of at most 0.013.
Values may be sent and summed in bfloat16 or wider, within the bound.
A program may use at most 64 MiB of HBM per device.

v0:
```python
import math

import jax
import jax.numpy as jnp
import numpy as np
from jax import lax
from jax.experimental import pallas as pl
from jax.experimental.pallas import tpu as pltpu
from jax.sharding import PartitionSpec as P

MESH = pl.DeviceIdType.MESH
F32 = jnp.float32
BF16 = jnp.bfloat16

N = 2048
ROWS = 64
NR = 32
NB = 8
NCH = 2
TPC = 4 // NCH
FLOOR = 0.05
RT = math.sqrt(0.5)


def place(a):
    return 8 * (a % 4) + a // 4


def tables():
    q = np.arange(256)
    k1 = np.arange(8)
    th = 2 * np.pi * (q[None, :] * k1[:, None] % 2048) / 2048
    tw1 = np.stack([np.cos(th), -np.sin(th)]) / math.sqrt(8.0)
    th = 2 * np.pi * (q[:, None] * q[None, :] % 256) / 256
    cos, sin = np.cos(th) / 16, np.sin(th) / 16
    w1 = np.empty((32, 2, 8, 2, 256))
    c3, s3 = cos.reshape(32, 8, 256), sin.reshape(32, 8, 256)
    w1[:, 0, :, 0], w1[:, 0, :, 1] = c3, s3
    w1[:, 1, :, 0], w1[:, 1, :, 1] = -s3, c3
    w4 = np.empty((32, 2, 8, 2, 256))
    w4[:, 0, :, 0], w4[:, 0, :, 1] = c3, s3
    w4[:, 1, :, 0], w4[:, 1, :, 1] = -s3, c3
    r = np.arange(64)
    th = 2 * np.pi * (r[:, None] * r[None, :] % 64) / 64
    cos, sin = np.cos(th) / 8, np.sin(th) / 8
    w2 = np.zeros((2, 2, 64, 2, 2, 64))
    w3 = np.zeros((2, 2, 64, 2, 2, 64))
    for x in range(2):
        w2[0, x, :, 0, x], w2[0, x, :, 1, x] = cos, -sin
        w2[1, x, :, 0, x], w2[1, x, :, 1, x] = sin, cos
        w3[0, x, :, 0, x], w3[0, x, :, 1, x] = cos, sin
        w3[1, x, :, 0, x], w3[1, x, :, 1, x] = -sin, cos
    a = np.arange(32)
    th = 2 * np.pi * (r[None, :] * a[:, None] % 2048) / 2048
    tw2 = np.empty((2, 32, 128))
    where = place(a)
    tw2[0, where] = np.tile(np.cos(th), (1, 2)) / math.sqrt(32.0)
    tw2[1, where] = np.tile(-np.sin(th), (1, 2)) / math.sqrt(32.0)
    p1 = np.zeros((256, 256))
    for m in range(8):
        p1[where * 8 + m, 32 * m + a] = 1
    p2 = np.zeros((2, 2, 4, 8, 2, 64))
    for c in range(2):
        for x in range(2):
            for t in range(4):
                for k in range(8):
                    p2[c, x, t, k, c, t + 4 * x + 8 * k] = 1
    bf = lambda v, *s: np.asarray(v.reshape(s), jnp.bfloat16)
    return (
        bf(w1, 512, 512),
        bf(w2, 256, 256),
        bf(w3, 256, 256),
        bf(w4, 512, 512),
        bf(p1, 256, 256),
        bf(p2, 128, 128),
        np.asarray(tw1, np.float32),
        np.asarray(tw2, np.float32),
    )


def add(x, y):
    return (x[0] + y[0], x[1] + y[1])


def sub(x, y):
    return (x[0] - y[0], x[1] - y[1])


def turn(x, s):
    return (-x[1], x[0]) if s > 0 else (x[1], -x[0])


def mul(x, c, d):
    return (x[0] * c - x[1] * d, x[0] * d + x[1] * c)


def mul_const(x, num, den, s):
    num %= den
    if num == 0:
        return x
    if 4 * num == den:
        return turn(x, s)
    if 2 * num == den:
        return (-x[0], -x[1])
    if 8 * num == den:
        r = F32(RT)
        return ((x[0] - s * x[1]) * r, (x[1] + s * x[0]) * r)
    if 8 * num == 3 * den:
        r = F32(RT)
        return ((-x[0] - s * x[1]) * r, (s * x[0] - x[1]) * r)
    th = 2 * math.pi * num / den
    return mul(x, F32(math.cos(th)), F32(s * math.sin(th)))


def dft4(x, s):
    t0, t1, t2, t3 = add(x[0], x[2]), sub(x[0], x[2]), add(x[1], x[3]), turn(sub(x[1], x[3]), s)
    return [add(t0, t2), add(t1, t3), sub(t0, t2), sub(t1, t3)]


def dft8(x, s):
    e, o = dft4(x[0::2], s), dft4(x[1::2], s)
    o = [mul_const(o[k], k, 8, s) for k in range(4)]
    return [add(e[k], o[k]) for k in range(4)] + [sub(e[k], o[k]) for k in range(4)]


def dft32_forward(x):
    cols = [dft4([x[8 * p1 + p0] for p1 in range(4)], -1) for p0 in range(8)]
    out = []
    for a0 in range(4):
        out += dft8([mul_const(cols[p0][a0], p0 * a0, 32, -1) for p0 in range(8)], -1)
    return out


def dft32_inverse(x):
    rows = [dft8(x[8 * a0 : 8 * a0 + 8], 1) for a0 in range(4)]
    out = [None] * 32
    for p0 in range(8):
        y = dft4([mul_const(rows[a0][p0], p0 * a0, 32, 1) for a0 in range(4)], 1)
        for p1 in range(4):
            out[8 * p1 + p0] = y[p1]
    return out


def dot(x, y, dims):
    return lax.dot_general(x, y, (dims, ((), ())), preferred_element_type=F32)


NN = ((1,), (0,))
NT = ((1,), (1,))


def kernel(
    model, dirty, pb, psf, offs, w1h, w2h, w3h, w4h, p1h, p2h, tw1h, tw2h,
    res_out, ret_out,
    model_v, dirty_v, pb_v, psf_v, w1, w2, w3, w4, p1, p2, tw1, tw2,
    z1, send1, recv1, send2, recv2, psfp, y_v, u_v, z2,
    pbf, sendw, recvw, send3, recv3, send4, recv4, buf, rden, joint, res_v, ret_v,
    lsem, osem, ssem, rsem,
):
    bme = lax.axis_index("beam")
    rme = lax.axis_index("row")
    yme, zme = rme // 8, rme % 8

    def row_peer(i):
        n = i // 4
        dz = 4 + (1 - 2 * (n % 2)) * ((n + 1) // 2)
        dy = 3 - i % 4
        return ((yme + dy) % 4) * 8 + (zme + dz) % 8

    def beam_peer(i):
        return (bme + 1 + i) % NB

    loads = [
        (model, model_v), (w1h, w1), (tw1h, tw1), (pb, pb_v), (psf, psf_v), (p1h, p1), (p2h, p2),
        (w2h, w2), (w3h, w3), (tw2h, tw2), (w4h, w4), (dirty, dirty_v),
    ]
    copies = [pltpu.make_async_copy(h, v, lsem.at[i]) for i, (h, v) in enumerate(loads)]
    for c in copies:
        c.start()

    barrier = pltpu.get_barrier_semaphore()

    def greet_row(i, _):
        pl.semaphore_signal(barrier, inc=1, device_id=(bme, row_peer(i)), device_id_type=MESH)
        return 0

    def greet_beam(i, _):
        pl.semaphore_signal(barrier, inc=1, device_id=(beam_peer(i), rme), device_id_type=MESH)
        return 0

    lax.fori_loop(0, NR - 1, greet_row, 0)
    lax.fori_loop(0, NB - 1, greet_beam, 0)

    copies[0].wait()
    copies[1].wait()
    copies[2].wait()
    for rb in range(4):
        for qt in range(2):
            rows = pl.ds(16 * rb, 16)
            x = [model_v[rows, pl.ds(256 * p + 128 * qt, 128)].astype(F32) for p in range(8)]
            a, b, c, d = x[1] - x[5], x[3] - x[7], x[0] - x[4], x[2] - x[6]
            s04, s26, s15, s37 = x[0] + x[4], x[2] + x[6], x[1] + x[5], x[3] + x[7]
            e0, o0 = s04 + s26, s15 + s37
            u, v = (a - b) * F32(RT), (a + b) * F32(RT)
            y1, y2, y3 = (c + u, -d - v), (s04 - s26, s37 - s15), (c - u, d - v)
            y = [(e0 + o0, None), y1, y2, y3, (e0 - o0, None), (y3[0], -y3[1]), (y2[0], -y2[1]), (y1[0], -y1[1])]
            for k in range(8):
                tc = tw1[0, pl.ds(k, 1), pl.ds(128 * qt, 128)]
                ts = tw1[1, pl.ds(k, 1), pl.ds(128 * qt, 128)]
                re, im = y[k]
                if im is None:
                    zr, zi = re * tc, re * ts
                else:
                    zr, zi = re * tc - im * ts, re * ts + im * tc
                to = pl.ds(64 * (k // 4) + 16 * rb, 16)
                z1[k % 4, to, pl.ds(128 * qt, 128)] = zr.astype(BF16)
                z1[k % 4, to, pl.ds(256 + 128 * qt, 128)] = zi.astype(BF16)

    def send_rows(phase, ch, src, dst):
        def go(i, _):
            peer = row_peer(i)
            pltpu.make_async_remote_copy(
                src_ref=src.at[ch, peer],
                dst_ref=dst.at[ch, rme],
                send_sem=ssem.at[phase * NCH + ch],
                recv_sem=rsem.at[phase * NCH + ch],
                device_id=(bme, peer),
                device_id_type=MESH,
            ).start()
            return 0

        lax.fori_loop(0, NR - 1, go, 0)
        dst[ch, rme] = src[ch, rme]

    def wait_rows(sems, phase, ch, dst):
        part = dst.at[ch, pl.ds(0, NR - 1)]
        pltpu.make_async_copy(part, part, sems.at[phase * NCH + ch]).wait()

    base = 2 * NCH

    def send_beam(which, peer, src, dst):
        pltpu.make_async_remote_copy(
            src_ref=src.at[peer],
            dst_ref=dst.at[bme],
            send_sem=ssem.at[base + which],
            recv_sem=rsem.at[base + which],
            device_id=(peer, rme),
            device_id_type=MESH,
        ).start()

    def wait_beam(sems, which, dst):
        part = dst.at[pl.ds(0, NB - 1)]
        pltpu.make_async_copy(part, part, sems.at[base + which]).wait()

    for ch in range(NCH):
        for i in range(TPC):
            t = ch * TPC + i
            out = dot(w1[...], z1[t], NT).astype(BF16)
            send1[ch, :, i] = out.reshape(NR, 16, 128)
        if ch == 0:
            pl.semaphore_wait(barrier, NR - 1 + NB - 1)
        send_rows(0, ch, send1, recv1)

    copies[3].wait()
    for rb in range(4):
        both = pb_v[pl.ds(16 * rb, 16), :].astype(F32)
        pbf[pl.ds(16 * rb, 16), :] = both
        for j in range(2):
            part = both[8 * j : 8 * j + 8]
            sendw[2 * rb + j] = jnp.concatenate([part[:, :1024], part[:, 1024:]], axis=0).astype(BF16)

    def go_w(i, _):
        send_beam(0, beam_peer(i), sendw, recvw)
        return 0

    lax.fori_loop(0, NB - 1, go_w, 0)
    recvw[bme] = sendw[bme]

    copies[4].wait()
    copies[5].wait()
    copies[6].wait()
    for m in range(8):
        part = psf_v[:, pl.ds(256 * m, 256)].astype(BF16)
        y_v[:, pl.ds(8 * m, 8), :] = dot(p1[...], part, NT).reshape(32, 8, 128)
    low = lax.broadcasted_iota(jnp.int32, (32, 128), 1) < 64
    for a in range(0, 32, 2):
        pair = y_v[pl.ds(a, 2)].reshape(128, 128).astype(BF16)
        got = dot(p2[...], pair, NT)
        for c in range(2):
            one, two = got[64 * c : 64 * c + 32], got[64 * c + 32 : 64 * c + 64]
            first = jnp.where(low, one, pltpu.roll(two, 64, 1))
            second = jnp.where(low, pltpu.roll(one, 64, 1), two)
            for t in range(4):
                psfp[t, c, pl.ds(8 * a, 8), :] = first[8 * t : 8 * t + 8]
                psfp[t, c, pl.ds(8 * a + 8, 8), :] = second[8 * t : 8 * t + 8]

    for b in range(NB):
        buf[b, pl.ds(0, 16)] = jnp.zeros((16, 8, 128), F32)
        buf[b, pl.ds(32, 16)] = jnp.zeros((16, 8, 128), F32)

    copies[7].wait()
    copies[8].wait()
    copies[9].wait()

    for ch in range(NCH):
        wait_rows(rsem, 0, ch, recv1)
        for i in range(TPC):
            t = ch * TPC + i
            x = []
            for p in range(NR):
                both = recv1[ch, p, i].astype(F32)
                x.append((both[:8], both[8:]))
            x = dft32_forward(x)
            for a in range(0, NR, 2):
                turned = [mul(x[a + j], tw2[0, pl.ds(a + j, 1), :], tw2[1, pl.ds(a + j, 1), :]) for j in range(2)]
                for c in range(2):
                    z2[pl.ds(8 * a, 16), pl.ds(128 * c, 128)] = jnp.concatenate(
                        [turned[0][c], turned[1][c]], axis=0
                    ).astype(BF16)
            f = dot(z2[...], w2[...], NN)
            fr, fi = f[:, :128], f[:, 128:]
            pr, pi = psfp[t, 0], psfp[t, 1]
            h = jnp.concatenate([(fr * pr - fi * pi).astype(BF16), (fr * pi + fi * pr).astype(BF16)], axis=1)
            g = dot(h, w3[...], NN)
            x = []
            for a in range(NR):
                gr, gi = g[8 * a : 8 * a + 8, :128], g[8 * a : 8 * a + 8, 128:]
                x.append(mul((gr, gi), tw2[0, pl.ds(a, 1), :], -tw2[1, pl.ds(a, 1), :]))
            x = dft32_inverse(x)
            for p in range(NR):
                send2[ch, p, i] = jnp.concatenate([x[p][0], x[p][1]], axis=0).astype(BF16)
        send_rows(1, ch, send2, recv2)

    def tile_sum(t):
        total = None
        for b in range(NB):
            one = buf[b, t - offs[b] + 16]
            total = one if total is None else total + one
        return total

    wait_beam(rsem, 0, recvw)
    for b in range(NB):
        for c in range(8):
            both = recvw[b, :, pl.ds(128 * c, 128)].astype(F32)
            both = both * both
            buf[b, 16 + c] = both[:8]
            buf[b, 24 + c] = both[8:]

    def weigh(t, _):
        rden[t] = 1.0 / jnp.maximum(tile_sum(t), FLOOR)
        return 0

    lax.fori_loop(0, 32, weigh, 0)

    copies[10].wait()
    for ch in range(NCH):
        wait_rows(rsem, 1, ch, recv2)
        for i in range(TPC):
            t = ch * TPC + i
            got = recv2[ch, :, i].reshape(512, 128)
            u_v[t] = dot(got.T, w4[...], NN)

    copies[11].wait()

    def last(i, _):
        rb = beam_peer(i)
        row0 = pl.multiple_of(8 * rb, 8)
        rows = pl.ds(row0, 8)
        for qt in range(2):
            v = []
            for k in range(8):
                at = pl.ds(pl.multiple_of(64 * (k // 4) + 8 * rb, 8), 8)
                ur = u_v[k % 4, at, pl.ds(128 * qt, 128)]
                ui = u_v[k % 4, at, pl.ds(256 + 128 * qt, 128)]
                tc = tw1[0, pl.ds(k, 1), pl.ds(128 * qt, 128)]
                ts = -tw1[1, pl.ds(k, 1), pl.ds(128 * qt, 128)]
                re = ur * tc - ui * ts
                v.append((re, None if k % 4 == 0 else ur * ts + ui * tc))
            s = [None] + [(v[k][0] + v[8 - k][0], v[k][1] - v[8 - k][1]) for k in (1, 2, 3)]
            pp, mm = v[0][0] + v[4][0], v[0][0] - v[4][0]
            e1, e2 = pp + s[2][0], pp - s[2][0]
            o1, o2 = mm - s[2][1], mm + s[2][1]
            f, g = s[1][0] + s[3][0], s[1][1] - s[3][1]
            u = F32(RT) * ((s[1][0] - s[1][1]) - (s[3][0] + s[3][1]))
            w = F32(RT) * ((s[1][0] + s[1][1]) - (s[3][0] - s[3][1]))
            conv = [e1 + f, o1 + u, e2 - g, o2 - w, e1 - f, o1 - u, e2 + g, o2 + w]
            weighted = []
            for p in range(8):
                cols = pl.ds(256 * p + 128 * qt, 128)
                one = dirty_v[rows, cols] - conv[p]
                res_v[rows, cols] = one
                weighted.append(pbf[rows, cols] * one)
            for p in range(4):
                send3[rb, :, pl.ds(256 * p + 128 * qt, 128)] = jnp.concatenate(
                    [weighted[p], weighted[p + 4]], axis=0
                ).astype(BF16)

        @pl.when(i < NB - 1)
        def _():
            send_beam(1, rb, send3, recv3)

        return 0

    lax.fori_loop(0, NB, last, 0)
    recv3[bme] = send3[bme]
    res_copy = pltpu.make_async_copy(res_v, res_out, osem.at[0])
    res_copy.start()

    wait_beam(rsem, 1, recv3)
    for b in range(NB):
        for c in range(8):
            both = recv3[b, :, pl.ds(128 * c, 128)].astype(F32)
            buf[b, 16 + c] = both[:8]
            buf[b, 24 + c] = both[8:]

    def join(t, _):
        joint[t] = tile_sum(t) * rden[t]
        return 0

    lax.fori_loop(0, 32, join, 0)

    def reply(i, _):
        b = beam_peer(i)
        off = offs[b]
        for c in range(8):
            send4[b, :, pl.ds(128 * c, 128)] = jnp.concatenate([joint[off + c], joint[off + 8 + c]], axis=0).astype(BF16)

        @pl.when(i < NB - 1)
        def _():
            send_beam(2, b, send4, recv4)

        return 0

    lax.fori_loop(0, NB, reply, 0)
    recv4[bme] = send4[bme]
    wait_beam(rsem, 2, recv4)
    for b in range(NB):
        for h in range(2):
            rows, cols = pl.ds(8 * b, 8), pl.ds(1024 * h, 1024)
            looked = recv4[b].astype(F32)[8 * h : 8 * h + 8]
            ret_v[rows, cols] = pbf[rows, cols] * looked
    ret_copy = pltpu.make_async_copy(ret_v, ret_out, osem.at[1])
    ret_copy.start()

    for ch in range(NCH):
        wait_rows(ssem, 0, ch, recv1)
        wait_rows(ssem, 1, ch, recv2)
    wait_beam(ssem, 0, recvw)
    wait_beam(ssem, 1, recv3)
    wait_beam(ssem, 2, recv4)
    res_copy.wait()
    ret_copy.wait()


def body(dirty, model, psf_spectrum, primary_beam, offsets):
    consts = [jnp.asarray(v) for v in tables()]
    psf = jnp.swapaxes(psf_spectrum[0], 1, 2).reshape(128, N)
    hbm = pl.BlockSpec(memory_space=pl.ANY)
    image = lambda dt: pltpu.VMEM((ROWS, N), dt)
    block = lambda: pltpu.VMEM((NCH, NR, TPC, 16, 128), BF16)
    beam = lambda: pltpu.VMEM((NB, 16, 1024), BF16)
    scratch = [
        image(BF16), image(F32), image(BF16), pltpu.VMEM((128, N), F32),
        *[pltpu.VMEM(v.shape, v.dtype) for v in consts],
        pltpu.VMEM((4, 128, 512), BF16), block(), block(), block(), block(),
        pltpu.VMEM((4, 2, 256, 128), F32), pltpu.VMEM((32, 64, 128), F32), pltpu.VMEM((4, 128, 512), F32),
        pltpu.VMEM((256, 256), BF16),
        image(F32), beam(), beam(), beam(), beam(), beam(), beam(),
        pltpu.VMEM((NB, 48, 8, 128), F32), pltpu.VMEM((32, 8, 128), F32), pltpu.VMEM((32, 8, 128), F32),
        image(F32), image(F32),
        pltpu.SemaphoreType.DMA((12,)), pltpu.SemaphoreType.DMA((2,)),
        pltpu.SemaphoreType.DMA((2 * NCH + 3,)), pltpu.SemaphoreType.DMA((2 * NCH + 3,)),
    ]
    residual, returned = pl.pallas_call(
        kernel,
        out_shape=[jax.ShapeDtypeStruct((ROWS, N), F32)] * 2,
        in_specs=[hbm] * 4 + [pl.BlockSpec(memory_space=pltpu.SMEM)] + [hbm] * 8,
        out_specs=[hbm] * 2,
        scratch_shapes=scratch,
        compiler_params=pltpu.CompilerParams(
            collective_id=0, has_side_effects=True, vmem_limit_bytes=48 * 1024 * 1024
        ),
    )(model[0], dirty[0], primary_beam[0], psf, offsets, *consts)
    return (residual[None], returned[None])


def solution(mesh):
    in_specs = (
        P("beam", "row", None),
        P("beam", "row", None),
        P("beam", None, None, "row"),
        P("beam", "row", None),
        P(),
    )
    out_specs = (P("beam", "row", None), P("beam", "row", None))
    return jax.shard_map(body, mesh=mesh, in_specs=in_specs, out_specs=out_specs, check_vma=False)
```

profile of v0, /device:TPU:1, one launch (start us, length us, event | category | flops | bytes accessed | tf_op | source)
XLA Modules:
  0.0 61.8 jit_solution(9878838252799232185)
XLA Ops:
  0.6 0.0 copy-start.10
  0.6 0.0 copy-start.11
  0.7 0.7 %copy-done.10 = f32[2,8,256]{2,1,0:T(8,128)S(1)} copy-done((f32[2,8,256]{2,1,0:T(8,128)S(1)}, f32[2,8,256]{2,1,0:T(8,128)}, u32[]{:S(2)}) %copy-start.10) | copy-done | bytes 16408
  1.4 0.0 copy-done.11
  1.4 0.0 copy-start
  1.4 1.0 %copy-done = bf16[512,512]{1,0:T(8,128)(2,1)S(1)} copy-done((bf16[512,512]{1,0:T(8,128)(2,1)S(1)}, bf16[512,512]{1,0:T(8,128)(2,1)}, u32[]{:S(2)}) %copy-start) | copy-done | bytes 524312
  2.4 0.0 copy-start.1
  2.4 1.2 %copy-done.1 = f32[1,2,2048,64]{2,3,1,0:T(8,128)S(1)} copy-done((f32[1,2,2048,64]{2,3,1,0:T(8,128)S(1)}, f32[1,2,2048,64]{2,3,1,0:T(8,128)}, u32[]{:S(2)}) %copy-start.1) | copy-done | bytes 1048600
  3.6 0.0 copy-start.2
  3.6 1.0 %copy-done.2 = f32[1,64,2048]{2,1,0:T(8,128)S(1)} copy-done((f32[1,64,2048]{2,1,0:T(8,128)S(1)}, f32[1,64,2048]{2,1,0:T(8,128)}, u32[]{:S(2)}) %copy-start.2) | copy-done | bytes 524312
  4.7 0.0 copy-start.3
  4.7 0.9 %copy-done.3 = bf16[1,64,2048]{2,1,0:T(8,128)(2,1)S(1)} copy-done((bf16[1,64,2048]{2,1,0:T(8,128)(2,1)S(1)}, bf16[1,64,2048]{2,1,0:T(8,128)(2,1)}, u32[]{:S(2)}) %copy-start.3) | copy-done | bytes 262168
  5.6 0.0 copy-start.4
  5.6 0.9 %copy-done.4 = bf16[1,64,2048]{2,1,0:T(8,128)(2,1)S(1)} copy-done((bf16[1,64,2048]{2,1,0:T(8,128)(2,1)S(1)}, bf16[1,64,2048]{2,1,0:T(8,128)(2,1)}, u32[]{:S(2)}) %copy-start.4) | copy-done | bytes 262168
  6.6 0.0 copy-start.5
  6.6 0.9 %copy-done.5 = bf16[256,256]{1,0:T(8,128)(2,1)S(1)} copy-done((bf16[256,256]{1,0:T(8,128)(2,1)S(1)}, bf16[256,256]{1,0:T(8,128)(2,1)}, u32[]{:S(2)}) %copy-start.5) | copy-done | bytes 131096
  7.5 0.0 copy-start.6
  7.5 0.9 %copy-done.6 = bf16[256,256]{1,0:T(8,128)(2,1)S(1)} copy-done((bf16[256,256]{1,0:T(8,128)(2,1)S(1)}, bf16[256,256]{1,0:T(8,128)(2,1)}, u32[]{:S(2)}) %copy-start.6) | copy-done | bytes 131096
  8.4 0.0 copy-start.7
  8.4 0.9 %copy-done.7 = bf16[256,256]{1,0:T(8,128)(2,1)S(1)} copy-done((bf16[256,256]{1,0:T(8,128)(2,1)S(1)}, bf16[256,256]{1,0:T(8,128)(2,1)}, u32[]{:S(2)}) %copy-start.7) | copy-done | bytes 131096
  9.3 0.0 copy-start.8
  9.3 0.8 %copy-done.8 = f32[2,32,128]{2,1,0:T(8,128)S(1)} copy-done((f32[2,32,128]{2,1,0:T(8,128)S(1)}, f32[2,32,128]{2,1,0:T(8,128)}, u32[]{:S(2)}) %copy-start.8) | copy-done | bytes 32792
  10.0 0.0 copy-start.9
  10.0 0.8 %copy-done.9 = bf16[128,128]{1,0:T(8,128)(2,1)S(1)} copy-done((bf16[128,128]{1,0:T(8,128)(2,1)S(1)}, bf16[128,128]{1,0:T(8,128)(2,1)}, u32[]{:S(2)}) %copy-start.9) | copy-done | bytes 32792
  10.8 49.4 %shard_map.140 = (f32[64,2048]{1,0:T(8,128)S(1)}, f32[64,2048]{1,0:T(8,128)S(1)}) custom-call(bf16[64,2048]{1,0:T(8,128)(2,1)S(1)} %bitcast.14, f32[64,2048]{1,0:T(8,128)S(1)} %bitcast.13, bf16[64,2048]{1,0:T(8,128)(2,1)S(1)} %bitcast.15, f32[128,2048]{1,0:T(8,128)S(1)} %bitcast.10, s32[8]{0:T(128)S(1)} %copy-done.11, bf16[512,512]{1,0:T(8,128)(2,1)S(1)} %copy-done, ...), custom_call_target="tpu_custom_call" | custom-call | tf_op jit(solution)/shard_map/pallas_call | solution.py:474
  60.2 0.8 %copy.17 = f32[1,64,2048]{2,1,0:T(8,128)} copy(f32[1,64,2048]{2,1,0:T(8,128)S(1)} %bitcast.12) | data formatting | bytes 1048576
  61.0 0.8 %copy.18 = f32[1,64,2048]{2,1,0:T(8,128)} copy(f32[1,64,2048]{2,1,0:T(8,128)S(1)} %bitcast.11) | data formatting | bytes 1048576
Async XLA Ops:
  0.6 0.7 %copy-start.10 = (f32[2,8,256]{2,1,0:T(8,128)S(1)}, f32[2,8,256]{2,1,0:T(8,128)}, u32[]{:S(2)}) copy-start(f32[2,8,256]{2,1,0:T(8,128)} %constant.19.clone.tw1h) | copy-start | bytes 49156
  0.6 0.7 %copy-start.11 = (s32[8]{0:T(128)S(1)}, s32[8]{0:T(128)}, u32[]{:S(2)}) copy-start(s32[8]{0:T(128)} %offs.1) | copy-start | bytes 100
  1.4 1.0 %copy-start = (bf16[512,512]{1,0:T(8,128)(2,1)S(1)}, bf16[512,512]{1,0:T(8,128)(2,1)}, u32[]{:S(2)}) copy-start(bf16[512,512]{1,0:T(8,128)(2,1)} %constant.14.clone.w1h.w4h) | copy-start | bytes 1572868
  2.4 1.2 %copy-start.1 = (f32[1,2,2048,64]{2,3,1,0:T(8,128)S(1)}, f32[1,2,2048,64]{2,3,1,0:T(8,128)}, u32[]{:S(2)}) copy-start(f32[1,2,2048,64]{2,3,1,0:T(8,128)} %param.15) | copy-start | bytes 3145732
  3.6 1.0 %copy-start.2 = (f32[1,64,2048]{2,1,0:T(8,128)S(1)}, f32[1,64,2048]{2,1,0:T(8,128)}, u32[]{:S(2)}) copy-start(f32[1,64,2048]{2,1,0:T(8,128)} %param.13) | copy-start | bytes 1572868
  4.7 0.9 %copy-start.3 = (bf16[1,64,2048]{2,1,0:T(8,128)(2,1)S(1)}, bf16[1,64,2048]{2,1,0:T(8,128)(2,1)}, u32[]{:S(2)}) copy-start(bf16[1,64,2048]{2,1,0:T(8,128)(2,1)} %param.14) | copy-start | bytes 786436
  5.6 0.9 %copy-start.4 = (bf16[1,64,2048]{2,1,0:T(8,128)(2,1)S(1)}, bf16[1,64,2048]{2,1,0:T(8,128)(2,1)}, u32[]{:S(2)}) copy-start(bf16[1,64,2048]{2,1,0:T(8,128)(2,1)} %param.16) | copy-start | bytes 786436
  6.6 0.9 %copy-start.5 = (bf16[256,256]{1,0:T(8,128)(2,1)S(1)}, bf16[256,256]{1,0:T(8,128)(2,1)}, u32[]{:S(2)}) copy-start(bf16[256,256]{1,0:T(8,128)(2,1)} %constant.17.clone.p1h) | copy-start | bytes 393220
  7.5 0.9 %copy-start.6 = (bf16[256,256]{1,0:T(8,128)(2,1)S(1)}, bf16[256,256]{1,0:T(8,128)(2,1)}, u32[]{:S(2)}) copy-start(bf16[256,256]{1,0:T(8,128)(2,1)} %constant.16.clone.w3h) | copy-start | bytes 393220
  8.4 0.9 %copy-start.7 = (bf16[256,256]{1,0:T(8,128)(2,1)S(1)}, bf16[256,256]{1,0:T(8,128)(2,1)}, u32[]{:S(2)}) copy-start(bf16[256,256]{1,0:T(8,128)(2,1)} %constant.15.clone.w2h) | copy-start | bytes 393220
  9.3 0.8 %copy-start.8 = (f32[2,32,128]{2,1,0:T(8,128)S(1)}, f32[2,32,128]{2,1,0:T(8,128)}, u32[]{:S(2)}) copy-start(f32[2,32,128]{2,1,0:T(8,128)} %constant.20.clone.tw2h) | copy-start | bytes 98308
  10.0 0.8 %copy-start.9 = (bf16[128,128]{1,0:T(8,128)(2,1)S(1)}, bf16[128,128]{1,0:T(8,128)(2,1)}, u32[]{:S(2)}) copy-start(bf16[128,128]{1,0:T(8,128)(2,1)} %constant.18.clone.p2h) | copy-start | bytes 98308
where the time goes:
time: 62.3 us; the launch traced here: 61.8 us
  Pallas kernels  49.4 us (79%)
  local copies, waits for them, and re-layouts  11.7 us (19%)
  between operations  0.67 us (1%)
    pallas_call x1, Pallas kernels, body(): pl.pallas_call(kernel, out_shape=[jax.ShapeDtypeStruct((ROWS, N), F32)] *...  49.4 us
    unnamed x26, local copies, waits for them, and re-layouts  11.7 us

commit v1 on v0

v1 whole, which is shorter than its diff:
```python
import math

import jax
import jax.numpy as jnp
import numpy as np
from jax import lax
from jax.experimental import pallas as pl
from jax.experimental.pallas import tpu as pltpu
from jax.sharding import PartitionSpec as P

MESH = pl.DeviceIdType.MESH
F32 = jnp.float32
BF16 = jnp.bfloat16

N = 2048
ROWS = 64
NR = 32
NB = 8
FIRST = (0, 2, 1, 3)
FLOOR = 0.05
RT = math.sqrt(0.5)


def place(a):
    return 8 * (a % 4) + a // 4


def tables():
    q = np.arange(256)
    k1 = np.arange(8)
    th = 2 * np.pi * (q[None, :] * k1[:, None] % 2048) / 2048
    tw1 = np.stack([np.cos(th), -np.sin(th)]) / math.sqrt(8.0)
    th = 2 * np.pi * (q[:, None] * q[None, :] % 256) / 256
    cos, sin = np.cos(th) / 16, np.sin(th) / 16
    w1 = np.empty((32, 2, 8, 2, 256))
    c3, s3 = cos.reshape(32, 8, 256), sin.reshape(32, 8, 256)
    w1[:, 0, :, 0], w1[:, 0, :, 1] = c3, s3
    w1[:, 1, :, 0], w1[:, 1, :, 1] = -s3, c3
    w4 = np.empty((32, 2, 8, 2, 256))
    w4[:, 0, :, 0], w4[:, 0, :, 1] = c3, s3
    w4[:, 1, :, 0], w4[:, 1, :, 1] = -s3, c3
    r = np.arange(64)
    th = 2 * np.pi * (r[:, None] * r[None, :] % 64) / 64
    cos, sin = np.cos(th) / 8, np.sin(th) / 8
    w2 = np.zeros((2, 2, 64, 2, 2, 64))
    w3 = np.zeros((2, 2, 2, 64, 2, 2, 2, 2, 32))
    for x in range(2):
        w2[0, x, :, 0, x], w2[0, x, :, 1, x] = cos, -sin
        w2[1, x, :, 0, x], w2[1, x, :, 1, x] = sin, cos
        for t in range(2):
            for hi in range(2):
                part = slice(32 * hi, 32 * hi + 32)
                w3[t, 0, x, :, hi, 0, t, x], w3[t, 0, x, :, hi, 1, t, x] = cos[:, part], sin[:, part]
                w3[t, 1, x, :, hi, 0, t, x], w3[t, 1, x, :, hi, 1, t, x] = -sin[:, part], cos[:, part]
    a = np.arange(32)
    th = 2 * np.pi * (r[None, :] * a[:, None] % 2048) / 2048
    tw2 = np.empty((2, 32, 128))
    where = place(a)
    tw2[0, where] = np.tile(np.cos(th), (1, 2)) / math.sqrt(32.0)
    tw2[1, where] = np.tile(-np.sin(th), (1, 2)) / math.sqrt(32.0)
    tw3 = np.empty((2, 2, 32, 128))
    for hi in range(2):
        part = th[:, 32 * hi : 32 * hi + 32]
        tw3[hi, 0, where] = np.tile(np.cos(part), (1, 4)) / math.sqrt(32.0)
        tw3[hi, 1, where] = np.tile(np.sin(part), (1, 4)) / math.sqrt(32.0)
    p1 = np.zeros((256, 256))
    for m in range(8):
        p1[where * 8 + m, 32 * m + a] = 1
    p2 = np.zeros((2, 2, 4, 8, 2, 64))
    for c in range(2):
        for x in range(2):
            for t in range(4):
                for k in range(8):
                    p2[c, x, t, k, c, FIRST[t] + 4 * x + 8 * k] = 1
    bf = lambda v, *s: np.asarray(v.reshape(s), jnp.bfloat16)
    return (
        bf(w1, 512, 512),
        bf(w2, 256, 256),
        bf(w3, 512, 512),
        bf(w4, 512, 512),
        bf(p1, 256, 256),
        bf(p2, 128, 128),
        np.asarray(tw1, np.float32),
        np.asarray(tw2, np.float32),
        np.asarray(tw3, np.float32),
    )


def add(x, y):
    return (x[0] + y[0], x[1] + y[1])


def sub(x, y):
    return (x[0] - y[0], x[1] - y[1])


def turn(x, s):
    return (-x[1], x[0]) if s > 0 else (x[1], -x[0])


def mul(x, c, d):
    return (x[0] * c - x[1] * d, x[0] * d + x[1] * c)


def mul_const(x, num, den, s):
    num %= den
    if num == 0:
        return x
    if 4 * num == den:
        return turn(x, s)
    if 2 * num == den:
        return (-x[0], -x[1])
    if 8 * num == den:
        r = F32(RT)
        return ((x[0] - s * x[1]) * r, (x[1] + s * x[0]) * r)
    if 8 * num == 3 * den:
        r = F32(RT)
        return ((-x[0] - s * x[1]) * r, (s * x[0] - x[1]) * r)
    th = 2 * math.pi * num / den
    return mul(x, F32(math.cos(th)), F32(s * math.sin(th)))


def dft4(x, s):
    t0, t1, t2, t3 = add(x[0], x[2]), sub(x[0], x[2]), add(x[1], x[3]), turn(sub(x[1], x[3]), s)
    return [add(t0, t2), add(t1, t3), sub(t0, t2), sub(t1, t3)]


def dft8(x, s):
    e, o = dft4(x[0::2], s), dft4(x[1::2], s)
    o = [mul_const(o[k], k, 8, s) for k in range(4)]
    return [add(e[k], o[k]) for k in range(4)] + [sub(e[k], o[k]) for k in range(4)]


def dft32_forward(x):
    cols = [dft4([x[8 * p1 + p0] for p1 in range(4)], -1) for p0 in range(8)]
    out = []
    for a0 in range(4):
        out += dft8([mul_const(cols[p0][a0], p0 * a0, 32, -1) for p0 in range(8)], -1)
    return out


def dft32_inverse(x):
    rows = [dft8(x[8 * a0 : 8 * a0 + 8], 1) for a0 in range(4)]
    out = [None] * 32
    for p0 in range(8):
        y = dft4([mul_const(rows[a0][p0], p0 * a0, 32, 1) for a0 in range(4)], 1)
        for p1 in range(4):
            out[8 * p1 + p0] = y[p1]
    return out


def dot(x, y, dims):
    return lax.dot_general(x, y, (dims, ((), ())), preferred_element_type=F32)


NN = ((1,), (0,))
NT = ((1,), (1,))


def kernel(
    model, dirty, pb, psf, offs_h, w1h, w2h, w3h, w4h, p1h, p2h, tw1h, tw2h, tw3h,
    res_out, looked,
    model_v, dirty_v, pb_v, psf_v, w1, w2, w3, w4, p1, p2, tw1, tw2, tw3, offs,
    z1, send1, recv1, send2, recv2, psfp, y_v, u_v, z2,
    pbf, sendw, recvw, send3, recv3, send4, buf, rden, joint, res_v,
    lsem, osem, s1, r1, s2, r2, sb, rb_,
):
    bme = lax.axis_index("beam")
    rme = lax.axis_index("row")
    yme, zme = lax.div(rme, 8), lax.rem(rme, 8)
    pair, side = lax.div(bme, 2), lax.rem(bme, 2)

    def row_peer(i):
        dy, dz = (2, 1, 3, 0)[i // 8], (4, 3, 5, 2, 6, 1, 7, 0)[i % 8]
        return lax.rem(yme + dy, 4) * 8 + lax.rem(zme + dz, 8)

    def beam_peer(i):
        return lax.rem(bme + 1 + i, NB)

    def first_row(b):
        return pl.multiple_of(32 * lax.rem(b, 2) + 8 * lax.div(b, 2), 8)

    loads = [
        (model, model_v), (w1h, w1), (tw1h, tw1), (pb, pb_v), (psf, psf_v), (p1h, p1), (p2h, p2),
        (w2h, w2), (w3h, w3), (tw2h, tw2), (w4h, w4), (dirty, dirty_v), (tw3h, tw3), (offs_h, offs),
    ]
    copies = [pltpu.make_async_copy(h, v, lsem.at[i]) for i, (h, v) in enumerate(loads)]
    for c in copies[:3]:
        c.start()

    barrier = pltpu.get_barrier_semaphore()

    for i in range(NR - 1):
        pl.semaphore_signal(barrier, inc=1, device_id=(bme, row_peer(i)), device_id_type=MESH)
    for i in range(NB - 1):
        pl.semaphore_signal(barrier, inc=1, device_id=(beam_peer(i), rme), device_id_type=MESH)
    for c in copies[3:]:
        c.start()

    def send_rows(src, dst, ssem, rsem):
        for i in range(NR - 1):
            peer = row_peer(i)
            pltpu.make_async_remote_copy(
                src_ref=src.at[peer],
                dst_ref=dst.at[rme],
                send_sem=ssem,
                recv_sem=rsem,
                device_id=(bme, peer),
                device_id_type=MESH,
            ).start()
        dst[rme] = src[rme]

    def wait_bytes(part, sem):
        pltpu.make_async_copy(part, part, sem).wait()

    def send_beam(peer, src, dst, ssem, rsem):
        pltpu.make_async_remote_copy(
            src_ref=src,
            dst_ref=dst,
            send_sem=ssem,
            recv_sem=rsem,
            device_id=(peer, rme),
            device_id_type=MESH,
        ).start()

    copies[0].wait()
    copies[1].wait()
    copies[2].wait()
    for half in range(2):
        for rb in range(4):
            for qt in range(2):
                rows = pl.ds(16 * rb, 16)
                x = [model_v[rows, pl.ds(256 * p + 128 * qt, 128)].astype(F32) for p in range(8)]
                if half == 0:
                    s04, s26, s15, s37 = x[0] + x[4], x[2] + x[6], x[1] + x[5], x[3] + x[7]
                    e0, o0 = s04 + s26, s15 + s37
                    y2 = (s04 - s26, s37 - s15)
                    y = {0: (e0 + o0, None), 2: y2, 4: (e0 - o0, None), 6: (y2[0], -y2[1])}
                else:
                    a, b, c, d = x[1] - x[5], x[3] - x[7], x[0] - x[4], x[2] - x[6]
                    u, v = (a - b) * F32(RT), (a + b) * F32(RT)
                    y1, y3 = (c + u, -d - v), (c - u, d - v)
                    y = {1: y1, 3: y3, 5: (y3[0], -y3[1]), 7: (y1[0], -y1[1])}
                for k, (re, im) in y.items():
                    tc = tw1[0, pl.ds(k, 1), pl.ds(128 * qt, 128)]
                    ts = tw1[1, pl.ds(k, 1), pl.ds(128 * qt, 128)]
                    if im is None:
                        zr, zi = re * tc, re * ts
                    else:
                        zr, zi = re * tc - im * ts, re * ts + im * tc
                    to = pl.ds(128 * (FIRST.index(k % 4) % 2) + 64 * (k // 4) + 16 * rb, 16)
                    z1[half, to, pl.ds(128 * qt, 128)] = zr.astype(BF16)
                    z1[half, to, pl.ds(256 + 128 * qt, 128)] = zi.astype(BF16)
        out = dot(w1[...], z1[half], NT).astype(BF16)
        for i in range(2):
            send1[half, :, i] = out[:, 128 * i : 128 * i + 128].reshape(NR, 16, 128)
        if half == 0:
            pl.semaphore_wait(barrier, NR - 1 + NB - 1)
        send_rows(send1.at[half], recv1.at[half], s1.at[half], r1.at[half])

    copies[3].wait()
    for g in range(4):
        both = pb_v[pl.ds(16 * g, 16), :].astype(F32)
        pbf[pl.ds(16 * g, 16), :] = both
        for j in range(2):
            part = both[8 * j : 8 * j + 8]
            to = 2 * ((2 * g + j) % 4) + (2 * g + j) // 4
            sendw[to] = jnp.concatenate([part[:, :1024], part[:, 1024:]], axis=0).astype(BF16)

    for i in range(NB - 1):
        peer = beam_peer(i)
        send_beam(peer, sendw.at[peer], recvw.at[bme], sb.at[0], rb_.at[0])
    recvw[bme] = sendw[bme]

    copies[4].wait()
    copies[5].wait()
    copies[6].wait()
    for m in range(8):
        part = psf_v[:, pl.ds(256 * m, 256)].astype(BF16)
        y_v[:, pl.ds(8 * m, 8), :] = dot(p1[...], part, NT).reshape(32, 8, 128)
    low = lax.broadcasted_iota(jnp.int32, (32, 128), 1) < 64
    for a in range(0, 32, 2):
        two = y_v[pl.ds(a, 2)].reshape(128, 128).astype(BF16)
        got = dot(p2[...], two, NT)
        for c in range(2):
            one, two = got[64 * c : 64 * c + 32], got[64 * c + 32 : 64 * c + 64]
            first = jnp.where(low, one, pltpu.roll(two, 64, 1))
            second = jnp.where(low, pltpu.roll(one, 64, 1), two)
            for t in range(4):
                psfp[t, c, pl.ds(8 * a, 8), :] = first[8 * t : 8 * t + 8]
                psfp[t, c, pl.ds(8 * a + 8, 8), :] = second[8 * t : 8 * t + 8]

    for b in range(NB):
        buf[b, pl.ds(0, 16)] = jnp.zeros((16, 8, 128), F32)
        buf[b, pl.ds(32, 16)] = jnp.zeros((16, 8, 128), F32)

    copies[7].wait()
    copies[8].wait()
    copies[9].wait()
    copies[12].wait()
    copies[13].wait()

    def forward_columns(half, i):
        t = 2 * half + i
        x = []
        for p in range(NR):
            both = recv1[half, p, i].astype(F32)
            x.append((both[:8], both[8:]))
        x = dft32_forward(x)
        for a in range(0, NR, 2):
            turned = [mul(x[a + j], tw2[0, pl.ds(a + j, 1), :], tw2[1, pl.ds(a + j, 1), :]) for j in range(2)]
            for c in range(2):
                z2[t, pl.ds(8 * a, 16), pl.ds(128 * c, 128)] = jnp.concatenate(
                    [turned[0][c], turned[1][c]], axis=0
                ).astype(BF16)
        f = dot(z2[t], w2[...], NN)
        fr, fi = f[:, :128], f[:, 128:]
        pr, pi = psfp[t, 0], psfp[t, 1]
        return [(fr * pr - fi * pi).astype(BF16), (fr * pi + fi * pr).astype(BF16)]

    def inverse_columns(h, half, hi):
        g = dot(h, w3[:, pl.ds(256 * hi, 256)], NN)
        x = []
        for a in range(NR):
            gr, gi = g[8 * a : 8 * a + 8, :128], g[8 * a : 8 * a + 8, 128:]
            x.append(mul((gr, gi), tw3[hi, 0, pl.ds(a, 1), :], tw3[hi, 1, pl.ds(a, 1), :]))
        x = dft32_inverse(x)
        for p in range(NR):
            send2[hi, half, p] = jnp.concatenate([x[p][0], x[p][1]], axis=0).astype(BF16)

    def send_back(half, hi):
        send_rows(send2.at[hi, half], recv2.at[hi, half], s2.at[hi, half], r2.at[hi, half])

    for half in range(2):
        wait_bytes(recv1.at[half, pl.ds(0, NR - 1)], r1.at[half])
        h = jnp.concatenate(forward_columns(half, 0) + forward_columns(half, 1), axis=1)
        for hi in range(2):
            inverse_columns(h, half, hi)
            if half == 1 and hi == 1:
                wait_bytes(recv2.at[0, 1, pl.ds(0, NR - 1)], s2.at[0, 1])
            send_back(half, hi)

    def tile_sum(t):
        total = None
        for b in range(NB):
            one = buf[b, t - offs[b] + 16]
            total = one if total is None else total + one
        return total

    wait_bytes(recvw.at[pl.ds(0, NB - 1)], rb_.at[0])
    for b in range(NB):
        for c in range(8):
            both = recvw[b, :, pl.ds(128 * c, 128)].astype(F32)
            both = both * both
            buf[b, 16 + c] = both[:8]
            buf[b, 24 + c] = both[8:]

    def weigh(t, _):
        rden[t] = 1.0 / jnp.maximum(tile_sum(t), FLOOR)
        return 0

    lax.fori_loop(0, 32, weigh, 0)

    def last(hi, i):
        four = lax.rem(pair + 1 + i, 4)
        owner = 2 * four + hi
        row0 = first_row(owner)
        rows = pl.ds(row0, 8)
        for qt in range(2):
            v = []
            for k in range(8):
                t = FIRST.index(k % 4)
                at = pl.ds(pl.multiple_of(64 * (t % 2) + 32 * (k // 4) + 8 * four, 8), 8)
                ur = u_v[hi, t // 2, at, pl.ds(128 * qt, 128)]
                ui = u_v[hi, t // 2, at, pl.ds(256 + 128 * qt, 128)]
                tc = tw1[0, pl.ds(k, 1), pl.ds(128 * qt, 128)]
                ts = -tw1[1, pl.ds(k, 1), pl.ds(128 * qt, 128)]
                re = ur * tc - ui * ts
                v.append((re, None if k % 4 == 0 else ur * ts + ui * tc))
            s = [None] + [(v[k][0] + v[8 - k][0], v[k][1] - v[8 - k][1]) for k in (1, 2, 3)]
            pp, mm = v[0][0] + v[4][0], v[0][0] - v[4][0]
            e1, e2 = pp + s[2][0], pp - s[2][0]
            o1, o2 = mm - s[2][1], mm + s[2][1]
            f, g = s[1][0] + s[3][0], s[1][1] - s[3][1]
            u = F32(RT) * ((s[1][0] - s[1][1]) - (s[3][0] + s[3][1]))
            w = F32(RT) * ((s[1][0] + s[1][1]) - (s[3][0] - s[3][1]))
            conv = [e1 + f, o1 + u, e2 - g, o2 - w, e1 - f, o1 - u, e2 + g, o2 + w]
            weighted = []
            for p in range(8):
                cols = pl.ds(256 * p + 128 * qt, 128)
                one = dirty_v[rows, cols] - conv[p]
                res_v[rows, cols] = one
                weighted.append(pbf[rows, cols] * one)
            for p in range(4):
                send3[owner, :, pl.ds(256 * p + 128 * qt, 128)] = jnp.concatenate(
                    [weighted[p], weighted[p + 4]], axis=0
                ).astype(BF16)

        @pl.when(owner != bme)
        def _():
            send_beam(owner, send3.at[owner], recv3.at[bme], sb.at[1], rb_.at[1])

    kept = pltpu.make_async_copy(send4.at[bme], looked.at[bme], osem.at[2])

    def joint_rows():
        recv3[bme] = send3[bme]
        wait_bytes(recv3.at[pl.ds(0, NB - 1)], rb_.at[1])
        for b in range(NB):
            for c in range(8):
                both = recv3[b, :, pl.ds(128 * c, 128)].astype(F32)
                buf[b, 16 + c] = both[:8]
                buf[b, 24 + c] = both[8:]

        def join(t, _):
            joint[t] = tile_sum(t) * rden[t]
            return 0

        lax.fori_loop(0, 32, join, 0)

        def reply(i, _):
            b = lax.rem(bme + 1 + i, NB)
            off = offs[b]
            for c in range(8):
                send4[b, :, pl.ds(128 * c, 128)] = jnp.concatenate(
                    [joint[off + c], joint[off + 8 + c]], axis=0
                ).astype(BF16)

            @pl.when(i < NB - 1)
            def _():
                send_beam(b, send4.at[b], looked.at[bme], sb.at[2], rb_.at[2 + side])

            return 0

        lax.fori_loop(0, NB, reply, 0)
        kept.start()

    copies[10].wait()
    copies[11].wait()
    res_copies = []
    for hi in range(2):
        for half in range(2):
            wait_bytes(recv2.at[hi, half, pl.ds(0, NR - 1)], r2.at[hi, half])
            u_v[hi, half] = dot(recv2[hi, half].reshape(512, 128).T, w4[...], NN)

        def go_last(i, _, hi=hi):
            last(hi, i)
            return 0

        lax.fori_loop(0, 4, go_last, 0)
        rows = pl.ds(32 * hi, 32)
        res_copies.append(pltpu.make_async_copy(res_v.at[rows], res_out.at[rows], osem.at[hi]))
        res_copies[hi].start()

    joint_rows()

    for hi in range(2):
        for own, count in ((True, 3), (False, 4)):

            @pl.when((side == hi) == own)
            def _(hi=hi, count=count):
                wait_bytes(looked.at[pl.ds(0, count)], rb_.at[2 + hi])

    for half in range(2):
        wait_bytes(recv1.at[half, pl.ds(0, NR - 1)], s1.at[half])
    for hi, half in ((0, 0), (1, 0), (1, 1)):
        wait_bytes(recv2.at[hi, half, pl.ds(0, NR - 1)], s2.at[hi, half])
    for j in range(3):
        wait_bytes(recvw.at[pl.ds(0, NB - 1)], sb.at[j])
    for c in res_copies:
        c.wait()
    kept.wait()


def finish(res, looked, pb, res_out, ret_out, looked_v, pb_v, ret_v, res_v, isem, osem):
    ins = [
        pltpu.make_async_copy(looked, looked_v, isem.at[0]),
        pltpu.make_async_copy(pb, pb_v, isem.at[1]),
        pltpu.make_async_copy(res, res_v, isem.at[2]),
    ]
    for c in ins:
        c.start()
    ins[0].wait()
    ins[1].wait()
    outs = []
    for hi in range(2):
        for pair in range(2):
            both = pb_v[pl.ds(32 * hi + 16 * pair, 16), :].astype(F32)
            for j in range(2):
                four = 2 * pair + j
                seen = looked_v[2 * four + hi].astype(F32)
                for h in range(2):
                    cols = pl.ds(1024 * h, 1024)
                    ret_v[pl.ds(32 * hi + 8 * four, 8), cols] = (
                        both[8 * j : 8 * j + 8, 1024 * h : 1024 * h + 1024] * seen[8 * h : 8 * h + 8]
                    )
        rows = pl.ds(32 * hi, 32)
        outs.append(pltpu.make_async_copy(ret_v.at[rows], ret_out.at[rows], osem.at[hi]))
        outs[hi].start()
    ins[2].wait()
    outs.append(pltpu.make_async_copy(res_v, res_out, osem.at[2]))
    outs[2].start()
    for c in outs:
        c.wait()


def body(dirty, model, psf_spectrum, primary_beam, offsets):
    consts = [jnp.asarray(v) for v in tables()]
    psf = jnp.swapaxes(psf_spectrum[0], 1, 2).reshape(128, N)
    hbm = pl.BlockSpec(memory_space=pl.ANY)
    image = lambda dt: pltpu.VMEM((ROWS, N), dt)
    rows_in = lambda: pltpu.VMEM((2, NR, 2, 16, 128), BF16)
    rows_out = lambda: pltpu.VMEM((2, 2, NR, 16, 128), BF16)
    beam = lambda: pltpu.VMEM((NB, 16, 1024), BF16)
    scratch = [
        image(BF16), image(F32), image(BF16), pltpu.VMEM((128, N), F32),
        *[pltpu.VMEM(v.shape, v.dtype) for v in consts], pltpu.SMEM((NB,), jnp.int32),
        pltpu.VMEM((2, 256, 512), BF16), rows_in(), rows_in(), rows_out(), rows_out(),
        pltpu.VMEM((4, 2, 256, 128), F32), pltpu.VMEM((32, 64, 128), F32), pltpu.VMEM((2, 2, 128, 512), F32),
        pltpu.VMEM((4, 256, 256), BF16),
        image(F32), beam(), beam(), beam(), beam(), beam(),
        pltpu.VMEM((NB, 48, 8, 128), F32), pltpu.VMEM((32, 8, 128), F32), pltpu.VMEM((32, 8, 128), F32),
        image(F32),
        pltpu.SemaphoreType.DMA((14,)), pltpu.SemaphoreType.DMA((4,)),
        pltpu.SemaphoreType.DMA((2,)), pltpu.SemaphoreType.DMA((2,)),
        pltpu.SemaphoreType.DMA((2, 2)), pltpu.SemaphoreType.DMA((2, 2)),
        pltpu.SemaphoreType.DMA((3,)), pltpu.SemaphoreType.DMA((4,)),
    ]
    residual, looked = pl.pallas_call(
        kernel,
        out_shape=[jax.ShapeDtypeStruct((ROWS, N), F32), jax.ShapeDtypeStruct((NB, 16, 1024), BF16)],
        in_specs=[hbm] * 14,
        out_specs=[hbm] * 2,
        scratch_shapes=scratch,
        compiler_params=pltpu.CompilerParams(
            collective_id=0, has_side_effects=True, vmem_limit_bytes=60 * 1024 * 1024
        ),
    )(model[0], dirty[0], primary_beam[0], psf, offsets, *consts)
    residual, returned = pl.pallas_call(
        finish,
        out_shape=[jax.ShapeDtypeStruct((ROWS, N), F32)] * 2,
        in_specs=[hbm] * 3,
        out_specs=[hbm] * 2,
        scratch_shapes=[
            beam(), image(BF16), image(F32), image(F32),
            pltpu.SemaphoreType.DMA((3,)), pltpu.SemaphoreType.DMA((3,)),
        ],
        compiler_params=pltpu.CompilerParams(vmem_limit_bytes=60 * 1024 * 1024),
    )(residual, looked, primary_beam[0])
    return (residual[None], returned[None])


def solution(mesh):
    in_specs = (
        P("beam", "row", None),
        P("beam", "row", None),
        P("beam", None, None, "row"),
        P("beam", "row", None),
        P(),
    )
    out_specs = (P("beam", "row", None), P("beam", "row", None))
    return jax.shard_map(body, mesh=mesh, in_specs=in_specs, out_specs=out_specs, check_vma=False)
```

time: 62.3 us -> 49.2 us (0.79)
  local copies, waits for them, and re-layouts: 11.7 us -> 0 us
  Pallas kernels: 49.4 us -> 48.4 us
    unnamed x26 -> x0, local copies, waits for them, and re-layouts: 11.7 us -> none
    pallas_call x1 -> x2, Pallas kernels: 49.4 us -> 48.4 us  [the longest x1 46.3 us: body(): pl.pallas_call(kernel, out_shape=[jax.ShapeDtypeStruct((ROWS, N), F32), j...]
where the time goes in v1:
time: 49.2 us; the launch traced here: 49 us
  Pallas kernels  48.4 us (98%)
  between operations  0.64 us (1%)
    pallas_call x1, Pallas kernels, body(): pl.pallas_call(kernel, out_shape=[jax.ShapeDtypeStruct((ROWS, N), F32), j...  46.3 us
    pallas_call x1, Pallas kernels, body(): pl.pallas_call(finish, out_shape=[jax.ShapeDtypeStruct((ROWS, N), F32)] *...  2.07 us

profile of v1, /device:TPU:1, one launch (start us, length us, event | category | flops | bytes accessed | tf_op | source)
XLA Modules:
  0.0 49.0 jit_solution(6425029225098799982)
XLA Ops:
  0.6 46.3 %shard_map.149 = (f32[64,2048]{1,0:T(8,128)}, bf16[8,16,1024]{2,1,0:T(8,128)(2,1)}) custom-call(bf16[64,2048]{1,0:T(8,128)(2,1)} %bitcast.14, f32[64,2048]{1,0:T(8,128)} %bitcast.13, bf16[64,2048]{1,0:T(8,128)(2,1)} %bitcast.10, f32[128,2048]{1,0:T(8,128)} %bitcast.12, s32[8]{0:T(128)} %offs_h.1, bf16[512,512]{1,0:T(8,128)(2,1)} %constant.16.clone.w1h.w4h, ...), custom_call_target="tpu_custom_call" | custom-call | tf_op jit(solution)/shard_map/pallas_call | solution.py:528
  47.0 2.1 %shard_map.150 = (f32[64,2048]{1,0:T(8,128)}, f32[64,2048]{1,0:T(8,128)}) custom-call(f32[64,2048]{1,0:T(8,128)} %get-tuple-element.6.res, bf16[8,16,1024]{2,1,0:T(8,128)(2,1)} %get-tuple-element.7.looked, bf16[64,2048]{1,0:T(8,128)(2,1)} %bitcast.11), custom_call_target="tpu_custom_call" | custom-call | tf_op jit(solution)/shard_map/pallas_call | solution.py:538

commit v2 on v1

--- a/solution.py
+++ b/solution.py
@@ -175,7 +175,8 @@
         return lax.rem(yme + dy, 4) * 8 + lax.rem(zme + dz, 8)
 
     def beam_peer(i):
-        return lax.rem(bme + 1 + i, NB)
+        chip = lax.rem(pair + (2, 2, 1, 1, 3, 3, 0, 0)[i], 4)
+        return 2 * chip + lax.rem(side + (1 + i) % 2, 2)
 
     def first_row(b):
         return pl.multiple_of(32 * lax.rem(b, 2) + 8 * lax.div(b, 2), 8)
@@ -340,12 +341,13 @@
                 wait_bytes(recv2.at[0, 1, pl.ds(0, NR - 1)], s2.at[0, 1])
             send_back(half, hi)
 
+    starts = [16 - offs[b] for b in range(NB)]
+
     def tile_sum(t):
-        total = None
-        for b in range(NB):
-            one = buf[b, t - offs[b] + 16]
-            total = one if total is None else total + one
-        return total
+        ones = [buf[b, starts[b] + t] for b in range(NB)]
+        while len(ones) > 1:
+            ones = [ones[k] + ones[k + 1] for k in range(0, len(ones), 2)]
+        return ones[0]
 
     wait_bytes(recvw.at[pl.ds(0, NB - 1)], rb_.at[0])
     for b in range(NB):
@@ -362,7 +364,7 @@
     lax.fori_loop(0, 32, weigh, 0)
 
     def last(hi, i):
-        four = lax.rem(pair + 1 + i, 4)
+        four = lax.rem(pair + (2, 1, 3, 0)[i], 4)
         owner = 2 * four + hi
         row0 = first_row(owner)
         rows = pl.ds(row0, 8)
@@ -411,27 +413,17 @@
                 buf[b, 16 + c] = both[:8]
                 buf[b, 24 + c] = both[8:]
 
-        def join(t, _):
+        for t in range(32):
             joint[t] = tile_sum(t) * rden[t]
-            return 0
-
-        lax.fori_loop(0, 32, join, 0)
-
-        def reply(i, _):
-            b = lax.rem(bme + 1 + i, NB)
+        for i in range(NB):
+            b = beam_peer(i)
             off = offs[b]
             for c in range(8):
                 send4[b, :, pl.ds(128 * c, 128)] = jnp.concatenate(
                     [joint[off + c], joint[off + 8 + c]], axis=0
                 ).astype(BF16)
-
-            @pl.when(i < NB - 1)
-            def _():
+            if i < NB - 1:
                 send_beam(b, send4.at[b], looked.at[bme], sb.at[2], rb_.at[2 + side])
-
-            return 0
-
-        lax.fori_loop(0, NB, reply, 0)
         kept.start()
 
     copies[10].wait()
@@ -442,11 +434,8 @@
             wait_bytes(recv2.at[hi, half, pl.ds(0, NR - 1)], r2.at[hi, half])
             u_v[hi, half] = dot(recv2[hi, half].reshape(512, 128).T, w4[...], NN)
 
-        def go_last(i, _, hi=hi):
+        for i in range(4):
             last(hi, i)
-            return 0
-
-        lax.fori_loop(0, 4, go_last, 0)
         rows = pl.ds(32 * hi, 32)
         res_copies.append(pltpu.make_async_copy(res_v.at[rows], res_out.at[rows], osem.at[hi]))
         res_copies[hi].start()

time: 49.2 us -> 48.2 us (0.980)
  Pallas kernels: 48.4 us -> 47.4 us
    pallas_call x1, Pallas kernels: 46.3 us -> 45.4 us  [body(): pl.pallas_call(kernel, out_shape=[jax.ShapeDtypeStruct((ROWS, N), F32), j...]
where the time goes in v2:
time: 48.2 us; the launch traced here: 48.1 us
  Pallas kernels  47.4 us (98%)
  between operations  0.64 us (1%)
    pallas_call x1, Pallas kernels, body(): pl.pallas_call(kernel, out_shape=[jax.ShapeDtypeStruct((ROWS, N), F32), j...  45.4 us
    pallas_call x1, Pallas kernels, body(): pl.pallas_call(finish, out_shape=[jax.ShapeDtypeStruct((ROWS, N), F32)] *...  2.07 us

profile of v2, /device:TPU:1, one launch (start us, length us, event | category | flops | bytes accessed | tf_op | source)
XLA Modules:
  0.0 48.1 jit_solution(8610081196159528783)
XLA Ops:
  0.6 45.4 %shard_map.149 = (f32[64,2048]{1,0:T(8,128)}, bf16[8,16,1024]{2,1,0:T(8,128)(2,1)}) custom-call(bf16[64,2048]{1,0:T(8,128)(2,1)} %bitcast.14, f32[64,2048]{1,0:T(8,128)} %bitcast.13, bf16[64,2048]{1,0:T(8,128)(2,1)} %bitcast.10, f32[128,2048]{1,0:T(8,128)} %bitcast.12, s32[8]{0:T(128)} %offs_h.1, bf16[512,512]{1,0:T(8,128)(2,1)} %constant.16.clone.w1h.w4h, ...), custom_call_target="tpu_custom_call" | custom-call | tf_op jit(solution)/shard_map/pallas_call | solution.py:517
  46.0 2.1 %shard_map.150 = (f32[64,2048]{1,0:T(8,128)}, f32[64,2048]{1,0:T(8,128)}) custom-call(f32[64,2048]{1,0:T(8,128)} %get-tuple-element.6.res, bf16[8,16,1024]{2,1,0:T(8,128)(2,1)} %get-tuple-element.7.looked, bf16[64,2048]{1,0:T(8,128)(2,1)} %bitcast.11), custom_call_target="tpu_custom_call" | custom-call | tf_op jit(solution)/shard_map/pallas_call | solution.py:527

commit v3 on v2

--- a/solution.py
+++ b/solution.py
@@ -159,10 +159,10 @@
 
 def kernel(
     model, dirty, pb, psf, offs_h, w1h, w2h, w3h, w4h, p1h, p2h, tw1h, tw2h, tw3h,
-    res_out, looked,
+    res_v, looked, pbf,
     model_v, dirty_v, pb_v, psf_v, w1, w2, w3, w4, p1, p2, tw1, tw2, tw3, offs,
     z1, send1, recv1, send2, recv2, psfp, y_v, u_v, z2,
-    pbf, sendw, recvw, send3, recv3, send4, buf, rden, joint, res_v,
+    sendw, recvw, send3, recv3, send4, buf, rden, joint,
     lsem, osem, s1, r1, s2, r2, sb, rb_,
 ):
     bme = lax.axis_index("beam")
@@ -402,7 +402,7 @@
         def _():
             send_beam(owner, send3.at[owner], recv3.at[bme], sb.at[1], rb_.at[1])
 
-    kept = pltpu.make_async_copy(send4.at[bme], looked.at[bme], osem.at[2])
+    kept = pltpu.make_async_copy(send4.at[bme], looked.at[bme], osem)
 
     def joint_rows():
         recv3[bme] = send3[bme]
@@ -428,7 +428,6 @@
 
     copies[10].wait()
     copies[11].wait()
-    res_copies = []
     for hi in range(2):
         for half in range(2):
             wait_bytes(recv2.at[hi, half, pl.ds(0, NR - 1)], r2.at[hi, half])
@@ -436,9 +435,6 @@
 
         for i in range(4):
             last(hi, i)
-        rows = pl.ds(32 * hi, 32)
-        res_copies.append(pltpu.make_async_copy(res_v.at[rows], res_out.at[rows], osem.at[hi]))
-        res_copies[hi].start()
 
     joint_rows()
 
@@ -455,39 +451,21 @@
         wait_bytes(recv2.at[hi, half, pl.ds(0, NR - 1)], s2.at[hi, half])
     for j in range(3):
         wait_bytes(recvw.at[pl.ds(0, NB - 1)], sb.at[j])
-    for c in res_copies:
-        c.wait()
     kept.wait()
 
 
-def finish(res, looked, pb, res_out, ret_out, looked_v, pb_v, ret_v, res_v, isem, osem):
-    ins = [
-        pltpu.make_async_copy(looked, looked_v, isem.at[0]),
-        pltpu.make_async_copy(pb, pb_v, isem.at[1]),
-        pltpu.make_async_copy(res, res_v, isem.at[2]),
-    ]
-    for c in ins:
-        c.start()
-    ins[0].wait()
-    ins[1].wait()
-    outs = []
+def finish(res, looked, pbf, res_out, ret_out, ret_v, osem):
+    outs = [pltpu.make_async_copy(res, res_out, osem.at[2])]
+    outs[0].start()
     for hi in range(2):
-        for pair in range(2):
-            both = pb_v[pl.ds(32 * hi + 16 * pair, 16), :].astype(F32)
-            for j in range(2):
-                four = 2 * pair + j
-                seen = looked_v[2 * four + hi].astype(F32)
-                for h in range(2):
-                    cols = pl.ds(1024 * h, 1024)
-                    ret_v[pl.ds(32 * hi + 8 * four, 8), cols] = (
-                        both[8 * j : 8 * j + 8, 1024 * h : 1024 * h + 1024] * seen[8 * h : 8 * h + 8]
-                    )
+        for four in range(4):
+            seen = looked[2 * four + hi].astype(F32)
+            for h in range(2):
+                rows, cols = pl.ds(32 * hi + 8 * four, 8), pl.ds(1024 * h, 1024)
+                ret_v[rows, cols] = pbf[rows, cols] * seen[8 * h : 8 * h + 8]
         rows = pl.ds(32 * hi, 32)
         outs.append(pltpu.make_async_copy(ret_v.at[rows], ret_out.at[rows], osem.at[hi]))
-        outs[hi].start()
-    ins[2].wait()
-    outs.append(pltpu.make_async_copy(res_v, res_out, osem.at[2]))
-    outs[2].start()
+        outs[1 + hi].start()
     for c in outs:
         c.wait()
 
@@ -496,6 +474,7 @@
     consts = [jnp.asarray(v) for v in tables()]
     psf = jnp.swapaxes(psf_spectrum[0], 1, 2).reshape(128, N)
     hbm = pl.BlockSpec(memory_space=pl.ANY)
+    vmem = pl.BlockSpec(memory_space=pltpu.VMEM)
     image = lambda dt: pltpu.VMEM((ROWS, N), dt)
     rows_in = lambda: pltpu.VMEM((2, NR, 2, 16, 128), BF16)
     rows_out = lambda: pltpu.VMEM((2, 2, NR, 16, 128), BF16)
@@ -506,35 +485,31 @@
         pltpu.VMEM((2, 256, 512), BF16), rows_in(), rows_in(), rows_out(), rows_out(),
         pltpu.VMEM((4, 2, 256, 128), F32), pltpu.VMEM((32, 64, 128), F32), pltpu.VMEM((2, 2, 128, 512), F32),
         pltpu.VMEM((4, 256, 256), BF16),
-        image(F32), beam(), beam(), beam(), beam(), beam(),
+        beam(), beam(), beam(), beam(), beam(),
         pltpu.VMEM((NB, 48, 8, 128), F32), pltpu.VMEM((32, 8, 128), F32), pltpu.VMEM((32, 8, 128), F32),
-        image(F32),
-        pltpu.SemaphoreType.DMA((14,)), pltpu.SemaphoreType.DMA((4,)),
+        pltpu.SemaphoreType.DMA((14,)), pltpu.SemaphoreType.DMA,
         pltpu.SemaphoreType.DMA((2,)), pltpu.SemaphoreType.DMA((2,)),
         pltpu.SemaphoreType.DMA((2, 2)), pltpu.SemaphoreType.DMA((2, 2)),
         pltpu.SemaphoreType.DMA((3,)), pltpu.SemaphoreType.DMA((4,)),
     ]
-    residual, looked = pl.pallas_call(
+    kept = pl.pallas_call(
         kernel,
-        out_shape=[jax.ShapeDtypeStruct((ROWS, N), F32), jax.ShapeDtypeStruct((NB, 16, 1024), BF16)],
+        out_shape=[pltpu.VMEM((ROWS, N), F32), pltpu.VMEM((NB, 16, 1024), BF16), pltpu.VMEM((ROWS, N), F32)],
         in_specs=[hbm] * 14,
-        out_specs=[hbm] * 2,
+        out_specs=[vmem] * 3,
         scratch_shapes=scratch,
         compiler_params=pltpu.CompilerParams(
-            collective_id=0, has_side_effects=True, vmem_limit_bytes=60 * 1024 * 1024
+            collective_id=0, has_side_effects=True, vmem_limit_bytes=56 * 1024 * 1024
         ),
     )(model[0], dirty[0], primary_beam[0], psf, offsets, *consts)
     residual, returned = pl.pallas_call(
         finish,
         out_shape=[jax.ShapeDtypeStruct((ROWS, N), F32)] * 2,
-        in_specs=[hbm] * 3,
+        in_specs=[vmem] * 3,
         out_specs=[hbm] * 2,
-        scratch_shapes=[
-            beam(), image(BF16), image(F32), image(F32),
-            pltpu.SemaphoreType.DMA((3,)), pltpu.SemaphoreType.DMA((3,)),
-        ],
-        compiler_params=pltpu.CompilerParams(vmem_limit_bytes=60 * 1024 * 1024),
-    )(residual, looked, primary_beam[0])
+        scratch_shapes=[image(F32), pltpu.SemaphoreType.DMA((3,))],
+        compiler_params=pltpu.CompilerParams(vmem_limit_bytes=56 * 1024 * 1024),
+    )(*[pltpu.with_memory_space_constraint(v, pltpu.VMEM) for v in kept])
     return (residual[None], returned[None])
 
 

time: 48.2 us -> 46.9 us (0.973)
  Pallas kernels: 47.4 us -> 46.2 us
    pallas_call x1, Pallas kernels: 2.07 us -> 0.99 us  [body(): pl.pallas_call(finish, out_shape=[jax.ShapeDtypeStruct((ROWS, N), F32)] *...]
where the time goes in v3:
time: 46.9 us
  Pallas kernels  46.2 us (99%)
  between operations  0.64 us (1%)
    pallas_call x1, Pallas kernels, body(): pl.pallas_call(kernel, out_shape=[pltpu.VMEM((ROWS, N), F32), pltpu.VMEM(...  45.2 us
    pallas_call x1, Pallas kernels, body(): pl.pallas_call(finish, out_shape=[jax.ShapeDtypeStruct((ROWS, N), F32)] *...  0.99 us

profile of v3, /device:TPU:1, one launch (start us, length us, event | category | flops | bytes accessed | tf_op | source)
XLA Modules:
  0.0 46.9 jit_solution(13498679000222631205)
XLA Ops:
  0.6 45.2 %shard_map.149 = (f32[64,2048]{1,0:T(8,128)S(1)}, bf16[8,16,1024]{2,1,0:T(8,128)(2,1)S(1)}, f32[64,2048]{1,0:T(8,128)S(1)}) custom-call(bf16[64,2048]{1,0:T(8,128)(2,1)} %bitcast.12, f32[64,2048]{1,0:T(8,128)} %bitcast.11, bf16[64,2048]{1,0:T(8,128)(2,1)} %bitcast.13, f32[128,2048]{1,0:T(8,128)} %bitcast.10, s32[8]{0:T(128)} %offs_h.1, ...), custom_call_target="tpu_custom_call" | custom-call | tf_op jit(solution)/shard_map/pallas_call | solution.py:495
  45.9 1.0 %shard_map.150 = (f32[64,2048]{1,0:T(8,128)}, f32[64,2048]{1,0:T(8,128)}) custom-call(f32[64,2048]{1,0:T(8,128)S(1)} %get-tuple-element.7.res, bf16[8,16,1024]{2,1,0:T(8,128)(2,1)S(1)} %get-tuple-element.8.looked, f32[64,2048]{1,0:T(8,128)S(1)} %get-tuple-element.9.pbf), custom_call_target="tpu_custom_call" | custom-call | tf_op jit(solution)/shard_map/pallas_call | solution.py:505

commit v4 on v3

--- a/solution.py
+++ b/solution.py
@@ -18,6 +18,8 @@
 NB = 8
 FIRST = (0, 2, 1, 3)
 FLOOR = 0.05
+FIRST_DONE = (0, 8, 1, 24)
+AHEAD, REST = 1, 2
 RT = math.sqrt(0.5)
 
 
@@ -198,9 +200,8 @@
     for c in copies[3:]:
         c.start()
 
-    def send_rows(src, dst, ssem, rsem):
-        for i in range(NR - 1):
-            peer = row_peer(i)
+    def send_rows(src, dst, ssem, rsem, part=None):
+        def send(peer):
             pltpu.make_async_remote_copy(
                 src_ref=src.at[peer],
                 dst_ref=dst.at[rme],
@@ -209,7 +210,21 @@
                 device_id=(bme, peer),
                 device_id_type=MESH,
             ).start()
-        dst[rme] = src[rme]
+
+        if part == AHEAD:
+            for peer in FIRST_DONE:
+                pl.when(rme != peer)(lambda peer=peer: send(peer))
+        if part != AHEAD:
+            for i in range(NR - 1):
+                peer = row_peer(i)
+                if part == REST:
+                    other = peer != FIRST_DONE[0]
+                    for one in FIRST_DONE[1:]:
+                        other &= peer != one
+                    pl.when(other)(lambda peer=peer: send(peer))
+                else:
+                    send(peer)
+            dst[rme] = src[rme]
 
     def wait_bytes(part, sem):
         pltpu.make_async_copy(part, part, sem).wait()
@@ -329,17 +344,23 @@
         for p in range(NR):
             send2[hi, half, p] = jnp.concatenate([x[p][0], x[p][1]], axis=0).astype(BF16)
 
-    def send_back(half, hi):
-        send_rows(send2.at[hi, half], recv2.at[hi, half], s2.at[hi, half], r2.at[hi, half])
+    def send_back(half, hi, part=None):
+        send_rows(send2.at[hi, half], recv2.at[hi, half], s2.at[hi, half], r2.at[hi, half], part)
 
     for half in range(2):
         wait_bytes(recv1.at[half, pl.ds(0, NR - 1)], r1.at[half])
         h = jnp.concatenate(forward_columns(half, 0) + forward_columns(half, 1), axis=1)
-        for hi in range(2):
-            inverse_columns(h, half, hi)
-            if half == 1 and hi == 1:
-                wait_bytes(recv2.at[0, 1, pl.ds(0, NR - 1)], s2.at[0, 1])
-            send_back(half, hi)
+        if half == 0:
+            for hi in range(2):
+                inverse_columns(h, half, hi)
+                send_back(half, hi)
+        else:
+            for hi in range(2):
+                inverse_columns(h, half, hi)
+                send_back(half, hi, AHEAD)
+            send_back(1, 0, REST)
+            wait_bytes(recv2.at[0, 1, pl.ds(0, NR - 1)], s2.at[0, 1])
+            send_back(1, 1, REST)
 
     starts = [16 - offs[b] for b in range(NB)]
 

time: 46.9 us -> 45.4 us (0.968)
  Pallas kernels: 46.2 us -> 44.6 us
    pallas_call x1, Pallas kernels: 45.2 us -> 43.6 us  [body(): pl.pallas_call(kernel, out_shape=[pltpu.VMEM((ROWS, N), F32), pltpu.VMEM(...]
where the time goes in v4:
time: 45.4 us; the launch traced here: 45.3 us
  Pallas kernels  44.6 us (98%)
  between operations  0.64 us (1%)
    pallas_call x1, Pallas kernels, body(): pl.pallas_call(kernel, out_shape=[pltpu.VMEM((ROWS, N), F32), pltpu.VMEM(...  43.6 us
    pallas_call x1, Pallas kernels, body(): pl.pallas_call(finish, out_shape=[jax.ShapeDtypeStruct((ROWS, N), F32)] *...  0.99 us

profile of v4, /device:TPU:1, one launch (start us, length us, event | category | flops | bytes accessed | tf_op | source)
XLA Modules:
  0.0 45.3 jit_solution(10194627975845557055)
XLA Ops:
  0.6 43.6 %shard_map.149 = (f32[64,2048]{1,0:T(8,128)S(1)}, bf16[8,16,1024]{2,1,0:T(8,128)(2,1)S(1)}, f32[64,2048]{1,0:T(8,128)S(1)}) custom-call(bf16[64,2048]{1,0:T(8,128)(2,1)} %bitcast.12, f32[64,2048]{1,0:T(8,128)} %bitcast.11, bf16[64,2048]{1,0:T(8,128)(2,1)} %bitcast.13, f32[128,2048]{1,0:T(8,128)} %bitcast.10, s32[8]{0:T(128)} %offs_h.1, ...), custom_call_target="tpu_custom_call" | custom-call | tf_op jit(solution)/shard_map/pallas_call | solution.py:516
  44.3 1.0 %shard_map.150 = (f32[64,2048]{1,0:T(8,128)}, f32[64,2048]{1,0:T(8,128)}) custom-call(f32[64,2048]{1,0:T(8,128)S(1)} %get-tuple-element.7.res, bf16[8,16,1024]{2,1,0:T(8,128)(2,1)S(1)} %get-tuple-element.8.looked, f32[64,2048]{1,0:T(8,128)S(1)} %get-tuple-element.9.pbf), custom_call_target="tpu_custom_call" | custom-call | tf_op jit(solution)/shard_map/pallas_call | solution.py:526

commit v5 on v4

--- a/solution.py
+++ b/solution.py
@@ -200,7 +200,7 @@
     for c in copies[3:]:
         c.start()
 
-    def send_rows(src, dst, ssem, rsem, part=None):
+    def send_rows(src, dst, ssem, rsem, part=None, ahead=()):
         def send(peer):
             pltpu.make_async_remote_copy(
                 src_ref=src.at[peer],
@@ -212,7 +212,7 @@
             ).start()
 
         if part == AHEAD:
-            for peer in FIRST_DONE:
+            for peer in ahead:
                 pl.when(rme != peer)(lambda peer=peer: send(peer))
         if part != AHEAD:
             for i in range(NR - 1):
@@ -344,8 +344,31 @@
         for p in range(NR):
             send2[hi, half, p] = jnp.concatenate([x[p][0], x[p][1]], axis=0).astype(BF16)
 
-    def send_back(half, hi, part=None):
-        send_rows(send2.at[hi, half], recv2.at[hi, half], s2.at[hi, half], r2.at[hi, half], part)
+    def send_back(half, hi, part=None, ahead=()):
+        send_rows(send2.at[hi, half], recv2.at[hi, half], s2.at[hi, half], r2.at[hi, half], part, ahead)
+
+    starts = [16 - offs[b] for b in range(NB)]
+
+    def tile_sum(t):
+        ones = [buf[b, starts[b] + t] for b in range(NB)]
+        while len(ones) > 1:
+            ones = [ones[k] + ones[k + 1] for k in range(0, len(ones), 2)]
+        return ones[0]
+
+    def weigh_all():
+        wait_bytes(recvw.at[pl.ds(0, NB - 1)], rb_.at[0])
+        for b in range(NB):
+            for c in range(8):
+                both = recvw[b, :, pl.ds(128 * c, 128)].astype(F32)
+                both = both * both
+                buf[b, 16 + c] = both[:8]
+                buf[b, 24 + c] = both[8:]
+
+        def weigh(t, _):
+            rden[t] = 1.0 / jnp.maximum(tile_sum(t), FLOOR)
+            return 0
+
+        lax.fori_loop(0, 32, weigh, 0)
 
     for half in range(2):
         wait_bytes(recv1.at[half, pl.ds(0, NR - 1)], r1.at[half])
@@ -354,35 +377,16 @@
             for hi in range(2):
                 inverse_columns(h, half, hi)
                 send_back(half, hi)
+            weigh_all()
         else:
             for hi in range(2):
                 inverse_columns(h, half, hi)
-                send_back(half, hi, AHEAD)
+            for peer in FIRST_DONE:
+                for hi in range(2):
+                    send_back(1, hi, AHEAD, (peer,))
             send_back(1, 0, REST)
             wait_bytes(recv2.at[0, 1, pl.ds(0, NR - 1)], s2.at[0, 1])
             send_back(1, 1, REST)
-
-    starts = [16 - offs[b] for b in range(NB)]
-
-    def tile_sum(t):
-        ones = [buf[b, starts[b] + t] for b in range(NB)]
-        while len(ones) > 1:
-            ones = [ones[k] + ones[k + 1] for k in range(0, len(ones), 2)]
-        return ones[0]
-
-    wait_bytes(recvw.at[pl.ds(0, NB - 1)], rb_.at[0])
-    for b in range(NB):
-        for c in range(8):
-            both = recvw[b, :, pl.ds(128 * c, 128)].astype(F32)
-            both = both * both
-            buf[b, 16 + c] = both[:8]
-            buf[b, 24 + c] = both[8:]
-
-    def weigh(t, _):
-        rden[t] = 1.0 / jnp.maximum(tile_sum(t), FLOOR)
-        return 0
-
-    lax.fori_loop(0, 32, weigh, 0)
 
     def last(hi, i):
         four = lax.rem(pair + (2, 1, 3, 0)[i], 4)

time: 45.4 us -> 45.3 us (level)
  no operation moved by 1% of the time
where the time goes in v5:
time: 45.3 us
  Pallas kernels  44.6 us (98%)
  between operations  0.64 us (1%)
    pallas_call x1, Pallas kernels, body(): pl.pallas_call(kernel, out_shape=[pltpu.VMEM((ROWS, N), F32), pltpu.VMEM(...  43.6 us
    pallas_call x1, Pallas kernels, body(): pl.pallas_call(finish, out_shape=[jax.ShapeDtypeStruct((ROWS, N), F32)] *...  0.99 us

profile of v5, /device:TPU:1, one launch (start us, length us, event | category | flops | bytes accessed | tf_op | source)
XLA Modules:
  0.0 45.3 jit_solution(7837325003906747673)
XLA Ops:
  0.6 43.6 %shard_map.149 = (f32[64,2048]{1,0:T(8,128)S(1)}, bf16[8,16,1024]{2,1,0:T(8,128)(2,1)S(1)}, f32[64,2048]{1,0:T(8,128)S(1)}) custom-call(bf16[64,2048]{1,0:T(8,128)(2,1)} %bitcast.12, f32[64,2048]{1,0:T(8,128)} %bitcast.11, bf16[64,2048]{1,0:T(8,128)(2,1)} %bitcast.13, f32[128,2048]{1,0:T(8,128)} %bitcast.10, s32[8]{0:T(128)} %offs_h.1, ...), custom_call_target="tpu_custom_call" | custom-call | tf_op jit(solution)/shard_map/pallas_call | solution.py:520
  44.3 1.0 %shard_map.150 = (f32[64,2048]{1,0:T(8,128)}, f32[64,2048]{1,0:T(8,128)}) custom-call(f32[64,2048]{1,0:T(8,128)S(1)} %get-tuple-element.7.res, bf16[8,16,1024]{2,1,0:T(8,128)(2,1)S(1)} %get-tuple-element.8.looked, f32[64,2048]{1,0:T(8,128)S(1)} %get-tuple-element.9.pbf), custom_call_target="tpu_custom_call" | custom-call | tf_op jit(solution)/shard_map/pallas_call | solution.py:530
